TPU v7x, 32 devices: a whole 2x2x4 slice. The times are simulated.
32 devices in a mesh: groups: 2 (over x), row: 16 (over z, y, core).
Axes of the slice: x: 2, y: 2, z: 4, core: 2. Of those that a mesh axis runs over, the one named last changes fastest.
Arguments:
- left_alignment: bfloat16 [64, 4096], P('groups', 'row'), parts along dimension 0, may hold values from -12 to 12
- right_alignment: bfloat16 [64, 4096], P('groups', 'row'), parts along dimension 0, may hold values from -12 to 12
- pair_update_gradient: bfloat16 [256, 128, 128], P(('groups', 'row')), parts along dimension 0, may hold values from -6 to 6
- weight: bfloat16 [1024, 128], replicated, may hold values from -0.1875 to 0.1875
- bias: bfloat16 [128], replicated, may hold values from -3 to 3
Outputs:
- pair_update: bfloat16 [256, 128, 128], P(('groups', 'row')), parts along dimension 0
- grad_left: float32 [64, 4096], P('groups', 'row'), parts along dimension 0
- grad_right: float32 [64, 4096], P('groups', 'row'), parts along dimension 0
- grad_weight: float32 [2048, 128], P('groups'), parts along dimension 0
- grad_bias: float32 [256], P('groups'), parts along dimension 0
There are 2 independent parts, one for each index of `groups`. A program takes and returns all parts, laid end to end along the dimension named above; an argument that names none is the same for every part. Nothing has to cross between parts.
All inputs are finite; a program needn't handle non-finite values.
Results may differ from a plain program's by a relative error of at most 0.0043.
Values may be sent and summed in bfloat16 or wider, within the bound.
A program may use at most 128 MiB of HBM per device.

v0:
```python
import jax
import jax.numpy as jnp
from jax import lax
from jax.sharding import PartitionSpec as P


def body(left_alignment, right_alignment, pair_update_gradient, weight, bias):
    sequence_count = left_alignment.shape[0]
    width = weight.shape[0]
    depth = weight.shape[1]
    shard_residues = pair_update_gradient.shape[0]
    grand_count = pair_update_gradient.shape[1]
    channel_total = left_alignment.shape[1] // shard_residues
    inv_seqs = 1.0 / sequence_count
    span = min(128, grand_count)
    count = grand_count // span
    left_shard_local = left_alignment.reshape(sequence_count, shard_residues, channel_total)
    right_collected = lax.all_gather(right_alignment, "row", axis=1, tiled=True)
    right_every = right_collected.reshape(sequence_count, grand_count, channel_total)
    bias_f = bias.astype(jnp.float32)

    def project_back(grad_rows):
        return lax.dot_general(
            grad_rows, weight, (((1,), (1,)), ((), ())), preferred_element_type=jnp.float32
        ).astype(jnp.bfloat16)

    def column_step(index, carry):
        pair_out, grad_left_acc, grad_right_acc, grad_weight_acc = carry
        offset = index * span
        right_blk = lax.dynamic_slice_in_dim(right_every, offset, span, 1)
        outer = jnp.einsum(
            "sic,sjd->ijcd", left_shard_local, right_blk, preferred_element_type=jnp.float32
        )
        outer = (outer * inv_seqs).astype(jnp.bfloat16).reshape(shard_residues * span, width)
        pair_blk = (jnp.dot(outer, weight, preferred_element_type=jnp.float32) + bias_f).astype(
            jnp.bfloat16
        )
        pair_out = lax.dynamic_update_slice_in_dim(
            pair_out, pair_blk.reshape(shard_residues, span, depth), offset, 1
        )
        grad_blk = lax.dynamic_slice_in_dim(pair_update_gradient, offset, span, 1).reshape(
            shard_residues * span, depth
        )
        inner = project_back(grad_blk).reshape(shard_residues, span, channel_total, channel_total)
        grad_left_acc = grad_left_acc + jnp.einsum(
            "ijcd,sjd->sic", inner, right_blk, preferred_element_type=jnp.float32
        )
        grad_weight_acc = grad_weight_acc + lax.dot_general(
            outer, grad_blk, (((0,), (0,)), ((), ())), preferred_element_type=jnp.float32
        )
        partial_blk = jnp.einsum(
            "ijcd,sic->sjd", inner, left_shard_local, preferred_element_type=jnp.float32
        )
        grad_right_acc = lax.dynamic_update_slice_in_dim(grad_right_acc, partial_blk, offset, 1)
        return (pair_out, grad_left_acc, grad_right_acc, grad_weight_acc)

    right_init = jnp.zeros((sequence_count, grand_count, channel_total), jnp.float32)
    initial = (
        jnp.zeros((shard_residues, grand_count, depth), jnp.bfloat16),
        jnp.zeros((sequence_count, shard_residues, channel_total), jnp.float32),
        right_init,
        jnp.zeros((width, depth), jnp.float32),
    )
    pair_out, grad_left_acc, grad_right_acc, grad_weight_acc = lax.fori_loop(
        0, count, column_step, initial
    )
    partial_rows = grad_right_acc.reshape(sequence_count, grand_count * channel_total)
    grad_right = lax.psum_scatter(partial_rows, "row", scatter_dimension=1, tiled=True) * inv_seqs
    bias_local = jnp.sum(pair_update_gradient, axis=(0, 1), dtype=jnp.float32)
    weight_total, bias_total = lax.psum((grad_weight_acc, bias_local), "row")
    inv_total = 1.0 / grand_count
    grad_left = (grad_left_acc * inv_seqs).reshape(sequence_count, shard_residues * channel_total)
    return (pair_out, grad_left, grad_right, weight_total * inv_total, bias_total * inv_total)


def solution(mesh):
    in_specs = (P("groups", "row"), P("groups", "row"), P(("groups", "row"), None, None), P(), P())
    out_specs = (
        P(("groups", "row"), None, None),
        P("groups", "row"),
        P("groups", "row"),
        P("groups", None),
        P("groups"),
    )
    return jax.shard_map(body, mesh=mesh, in_specs=in_specs, out_specs=out_specs, check_vma=False)
```

profile of v0, /device:TPU:1, one launch (start us, length us, event | category | flops | bytes accessed | tf_op | source)
XLA Modules:
  0.0 191.1 jit_solution(3599011914211065050)
XLA Ops:
  7.2 0.0 copy-start
  7.2 0.0 all-reduce.2.cloned.1.call-start
  7.2 0.9 reshape.40
  8.1 0.1 copy.16
  8.2 23.9 %all_gather.3 = bf16[32,4096]{1,0:T(8,128)(2,1)S(1)} all-gather(bf16[32,256]{1,0:T(8,128)(2,1)} %param.6), channel_id=1, replica_groups=mesh['groups'=2,'row'=16] {'row'}, dimensions={1}, use_global_device_ids=true | all-gather | bytes 278528 | tf_op jit(solution)/shard_map/all_gather | solution.py:18
  32.2 0.8 reshape.39
  33.0 0.5 copy.25
  33.5 0.7 fusion.6
  34.2 0.8 copy.17
  35.0 1.3 copy-done.1
  36.4 1.5 fusion
  37.9 0.0 all-reduce.2.cloned.1.call-update
  37.9 0.0 reduce-scatter.2.cloned.1.call-start
  38.0 1.7 convolution_convert_fusion
  39.7 0.1 copy.29
  39.8 2.6 %copy.18 = bf16[1024,1024]{0,1:T(8,128)(2,1)} copy(bf16[1024,1024]{1,0:T(8,128)(2,1)S(1)} %convolution_convert_fusion) | data formatting | bytes 4194304 | tf_op jit(solution)/shard_map/while/body/eval_jaxpr/convert_element_type | solution.py:25
  42.4 2.2 %copy.35 = bf16[128,8,8,128]{3,2,1,0:T(8,128)(2,1)S(1)} copy(bf16[128,8,8,128]{3,1,2,0:T(8,128)(2,1)} %bitcast.50) | data formatting | bytes 4194304
  44.6 1.3 convolution_bitcast_fusion
  45.9 3.0 %copy.23 = f32[32,128,32]{2,1,0:T(8,128)} copy(f32[32,128,32]{1,0,2:T(8,128)} %convolution_bitcast_fusion) | data formatting | bytes 1048576 | tf_op jit(solution)/shard_map/while/body/eval_jaxpr/ijcd,sic->sjd/dot_general | solution.py:51
  48.9 3.4 %reshape.46 = f32[32,4096]{1,0:T(8,128)} reshape(f32[32,128,32]{2,1,0:T(8,128)} %copy.23) | data formatting | bytes 1048576 | tf_op jit(solution)/shard_map/reshape | solution.py:67
  52.2 0.0 reduce-scatter.2.cloned.1.call-update
  52.3 1.2 copy.20
  53.5 1.7 fusion.13
  55.2 0.2 convert_reduce_fusion
  55.4 0.7 copy.24
  56.1 29.1 %psum.15 = f32[128]{0:T(128)S(1)} all-reduce(f32[128]{0:T(128)S(1)} %convert_reduce_fusion), channel_id=1, replica_groups=mesh['groups'=2,'row'=16] {'row'}, use_global_device_ids=true, to_apply=%region_3.0 | all-reduce | flops 128 | bytes 1024 | tf_op jit(solution)/shard_map/psum | solution.py:70
  85.2 0.5 broadcast_multiply_fusion.2
  85.7 3.1 %fusion.10 = bf16[1024,128]{1,0:T(8,128)(2,1)} fusion(bf16[1024,128]{1,0:T(8,128)(2,1)S(1)} %copy-done, bf16[128,8,8,128]{3,2,1,0:T(8,128)(2,1)} %bitcast.52, f32[128]{0:T(128)S(1)} %convert_element_type.23), kind=kOutput, calls=%fused_computation.11 | convolution fusion | flops 268697600 | bytes 2621952 | tf_op jit(solution)/shard_map/while/body/eval_jaxpr/dot_general | solution.py:35
  88.8 36.9 %all-reduce.2.cloned.1.call-done = f32[1024,128]{1,0:T(8,128)} async-done(((f32[1024,128]{1,0:T(8,128)}), f32[1024,128]{1,0:T(8,128)}) %all-reduce.2.cloned.1.call-update) | async-done | bytes 524304 | tf_op jit(solution)/shard_map/psum | solution.py:70
  125.6 1.9 broadcast_multiply_fusion
  127.5 55.4 %reduce-scatter.2.cloned.1.call-done = f32[32,256]{1,0:T(8,128)} async-done(((f32[32,4096]{1,0:T(8,128)}), f32[32,256]{1,0:T(8,128)}) %reduce-scatter.2.cloned.1.call-update) | async-done | bytes 32784 | tf_op jit(solution)/shard_map/reduce_scatter | solution.py:68
  182.9 1.4 broadcast_multiply_fusion.1
  (10 shorter events, 0.1 us)
Async XLA Ops:
  7.2 30.8 %copy-start = (bf16[1024,128]{1,0:T(8,128)(2,1)S(1)}, bf16[1024,128]{1,0:T(8,128)(2,1)}, u32[]{:S(2)}) copy-start(bf16[1024,128]{1,0:T(8,128)(2,1)} %param.8) | copy-start | bytes 786436
  7.2 118.4 %all-reduce.2.cloned.1.call-start = ((), (), s32[]{:S(2)}) async-start(), calls=%async_computation.2 | async-start | bytes 1048576 | tf_op jit(solution)/shard_map/psum | solution.py:70
  34.2 2.2 %copy-start.2 = (bf16[8,128,128]{2,1,0:T(8,128)(2,1)S(1)}, bf16[8,128,128]{2,1,0:T(8,128)(2,1)}, u32[]{:S(2)}) copy-start(bf16[8,128,128]{2,1,0:T(8,128)(2,1)} %param.7) | copy-start | bytes 786436
  35.0 1.4 copy-start.1
  37.9 145.0 %reduce-scatter.2.cloned.1.call-start = ((), (), s32[]{:S(2)}) async-start(), calls=%async_computation.1 | async-start | bytes 557056 | tf_op jit(solution)/shard_map/reduce_scatter | solution.py:68
  52.3 3.1 %copy-start.4 = (bf16[128]{0:T(256)(128)(2,1)S(1)}, bf16[128]{0:T(256)(128)(2,1)}, u32[]{:S(2)}) copy-start(bf16[128]{0:T(256)(128)(2,1)} %param.9) | copy-start | bytes 772
  53.5 1.7 copy-start.3
Sparse Core Ops, SparseCore 0:
  38.1 87.5 all-reduce.1
  129.2 53.7 reduce-scatter.1
where the time goes:
time: 194 us; the launch traced here: 191 us
  waiting for transfers between devices  92.3 us (48%)
  blocking collectives  53 us (27%)
  local copies, waits for them, and re-layouts  17.7 us (9%)
  between operations  14.2 us (7%)
  matrix products  9.89 us (5%)
  other arithmetic  3.94 us (2%)
    reduce_scatter x1, waiting for transfers between devices, body(): lax.psum_scatter(partial_rows, 'row', scatter_dimension=1, tiled=True)  55.4 us
    psum x1, waiting for transfers between devices, body(): weight_total, bias_total = lax.psum((grad_weight_acc, bias_local), 'row')  36.9 us
    psum x1, blocking collectives, body(): weight_total, bias_total = lax.psum((grad_weight_acc, bias_local), 'row')  29.1 us
    all_gather x1, blocking collectives, body(): right_collected = lax.all_gather(right_alignment, 'row', axis=1, tiled=True)  23.9 us
    unnamed x12, local copies, waits for them, and re-layouts  4.28 us
  transfers between devices with their start and end apart: 2, of which 2 were waited for; matrix products, arithmetic and copies ran while one was open for 12% of the time, Pallas kernels for 0%

commit v1 on v0

v1 whole, which is shorter than its diff:
```python
import functools

import jax
import jax.numpy as jnp
from jax import lax
from jax.experimental import pallas as pl
from jax.experimental.pallas import tpu as pltpu
from jax.sharding import PartitionSpec as P

F32, BF16 = jnp.float32, jnp.bfloat16
NN = (((1,), (0,)), ((), ()))
NT = (((1,), (1,)), ((), ()))
TN = (((0,), (0,)), ((), ()))


def dot(x, y, dims=NN):
    return lax.dot_general(x, y, dims, preferred_element_type=F32)


def kernel(
    n, left, right, grad, weight, bias,
    pair_out, gl_out, gr_out, gw_out, gb_out,
    weight_f, weight_r, t_mat, u_mat, u_acc,
    bt_all, gb_all, gr_send, gr_recv, gw_send, gw_recv, gw_all,
    bt_s, bt_r, gb_s, gb_r, gr_s, gr_r, gw_s, gw_r, ga_s, ga_r,
):
    seqs = left.shape[0]
    rows, residues, depth = grad.shape
    chans = left.shape[1] // rows
    inner = chans * seqs
    span = min(128, residues)
    blocks = residues // span
    me = lax.axis_index("row")

    def peer(k):
        return lax.rem(me + k, n)

    def each_peer(action):
        def step(k, carry):
            action(peer(k))
            return carry
        lax.fori_loop(1, n, step, 0)

    def each_block(action):
        if blocks == 1:
            action(0)
        else:
            def step(k, carry):
                action(pl.multiple_of(k * span, span))
                return carry
            lax.fori_loop(0, blocks, step, 0)

    def send(buffer_from, slot_from, buffer_to, sems, remote, p):
        pltpu.make_async_remote_copy(
            src_ref=buffer_from.at[slot_from],
            dst_ref=buffer_to.at[me],
            send_sem=sems.at[p],
            recv_sem=remote.at[me],
            device_id={"row": p},
            device_id_type=pl.DeviceIdType.MESH,
        ).start()

    def wait_recv(buffer, sems, remote, p):
        pltpu.make_async_remote_copy(
            src_ref=buffer.at[p],
            dst_ref=buffer.at[p],
            send_sem=sems.at[p],
            recv_sem=remote.at[p],
            device_id={"row": p},
            device_id_type=pl.DeviceIdType.MESH,
        ).wait_recv()

    def wait_send(buffer, sems, remote, slot, p):
        pltpu.make_async_remote_copy(
            src_ref=buffer.at[slot],
            dst_ref=buffer.at[slot],
            send_sem=sems.at[p],
            recv_sem=remote.at[p],
            device_id={"row": p},
            device_id_type=pl.DeviceIdType.MESH,
        ).wait_send()

    barrier = pltpu.get_barrier_semaphore()
    each_peer(lambda p: pl.semaphore_signal(
        barrier, inc=1, device_id={"row": p}, device_id_type=pl.DeviceIdType.MESH))

    lane_s = lax.broadcasted_iota(jnp.int32, (seqs, inner), 1) % seqs
    pick = (lane_s == lax.broadcasted_iota(jnp.int32, (seqs, inner), 0)).astype(BF16)
    lane_d = lax.broadcasted_iota(jnp.int32, (rows * chans, inner), 1) // seqs
    row_d = lax.broadcasted_iota(jnp.int32, (rows * chans, inner), 0) % chans
    own = lane_d == row_d
    spread = jnp.where(own, dot(right[...], pick, TN), 0.0)
    bt_all[me] = jnp.sum(spread.reshape(rows, chans, inner), axis=1).astype(BF16)

    gb = jnp.zeros((8, depth), F32)
    for i in range(rows):
        gb = gb + jnp.sum(grad[i].astype(F32).reshape(residues // 8, 8, depth), axis=0)
    gb_all[me] = gb

    pl.semaphore_wait(barrier, n - 1)

    def send_first(p):
        send(bt_all, me, bt_all, bt_s, bt_r, p)
        send(gb_all, me, gb_all, gb_s, gb_r, p)
    each_peer(send_first)

    a = jnp.concatenate([left[:, i * chans:(i + 1) * chans] for i in range(rows)], axis=0)
    weight_f[...] = weight[...].astype(F32)
    for d in range(chans):
        weight_r[:, d * depth:(d + 1) * depth] = weight_f[
            pl.ds(d, chans, stride=chans), :].astype(BF16)

    for d in range(chans):
        t = dot(a, weight_r[:, d * depth:(d + 1) * depth]).astype(BF16)
        for i in range(rows):
            t_mat[d * seqs:(d + 1) * seqs, i * depth:(i + 1) * depth] = (
                t[i * seqs:(i + 1) * seqs])

    def grad_of(start):
        return jnp.concatenate(
            [grad[i, pl.ds(start, span), :] for i in range(rows)], axis=1)

    scale = 1.0 / seqs

    def right_share(start):
        share = dot(grad_of(start), t_mat[...], NT) * scale
        gr_send[pl.ds(start // rows, span // rows)] = share.reshape(
            span // rows, rows, inner).astype(BF16)
    each_block(right_share)
    each_peer(lambda p: send(gr_send, p, gr_recv, gr_s, gr_r, p))

    each_peer(lambda p: wait_recv(bt_all, bt_s, bt_r, p))

    def right_of(start):
        return bt_all[pl.ds(start // rows, span // rows)].astype(F32).reshape(span, inner)

    def put_u(u):
        for d in range(chans):
            for i in range(rows):
                u_mat[i * seqs:(i + 1) * seqs, d * depth:(d + 1) * depth] = u[
                    d * seqs:(d + 1) * seqs, i * depth:(i + 1) * depth].astype(BF16)

    def u_of(start):
        return dot(right_of(start).T.astype(BF16), grad_of(start))

    if blocks == 1:
        put_u(u_of(0))
    else:
        u_acc[...] = jnp.zeros_like(u_acc)

        def add_u(start):
            u_acc[...] += u_of(start)
        each_block(add_u)
        put_u(u_acc)

    share_rows = gw_send.shape[1]
    a_t = a.astype(F32).T.astype(BF16)
    gw_scale = 1.0 / (seqs * residues)
    for d in range(chans):
        part = (dot(a_t, u_mat[:, d * depth:(d + 1) * depth]) * gw_scale)
        if share_rows >= chans:
            slot, off = divmod(d * chans, share_rows)
            gw_send[slot, off:off + chans, :] = part.astype(BF16)
        else:
            per = chans // share_rows
            gw_send[d * per:(d + 1) * per] = part.reshape(per, share_rows, depth).astype(BF16)
    each_peer(lambda p: send(gw_send, p, gw_recv, gw_s, gw_r, p))

    bias_f = jnp.broadcast_to(bias[...].astype(F32), (span, depth))

    def pair_of(start):
        pair = dot(right_of(start).astype(BF16), t_mat[...])
        for i in range(rows):
            pair_out[i, pl.ds(start, span), :] = (
                pair[:, i * depth:(i + 1) * depth] * scale + bias_f).astype(BF16)
    each_block(pair_of)

    each_peer(lambda p: wait_recv(gw_recv, gw_s, gw_r, p))
    gw_recv[me] = gw_send[me]
    total = lax.fori_loop(
        0, n, lambda k, acc: acc + gw_recv[k].astype(F32),
        jnp.zeros((share_rows, depth), F32))
    gw_all[me] = total.astype(BF16)
    each_peer(lambda p: send(gw_all, me, gw_all, ga_s, ga_r, p))

    gl = dot(u_mat[...], weight_r[...], NT) * scale
    for i in range(rows):
        gl_out[:, i * chans:(i + 1) * chans] = gl[i * seqs:(i + 1) * seqs]

    each_peer(lambda p: wait_recv(gr_recv, gr_s, gr_r, p))
    gr_recv[me] = gr_send[me]
    gr = lax.fori_loop(
        0, n, lambda k, acc: acc + gr_recv[k].astype(F32), jnp.zeros((rows, inner), F32))
    wide = jnp.broadcast_to(gr[:, None, :], (rows, chans, inner)).reshape(rows * chans, inner)
    wide = jnp.where(own, wide, 0.0)
    high = wide.astype(BF16)
    low = (wide - high.astype(F32)).astype(BF16)
    gr_out[...] = dot(pick, high, NT) + dot(pick, low, NT)

    each_peer(lambda p: wait_recv(gb_all, gb_s, gb_r, p))
    gb_total = lax.fori_loop(
        0, n, lambda k, acc: acc + gb_all[k], jnp.zeros((8, depth), F32))
    gb_out[...] = jnp.sum(gb_total, axis=0, keepdims=True) * (1.0 / residues)

    each_peer(lambda p: wait_recv(gw_all, ga_s, ga_r, p))
    for d in range(chans):
        if share_rows >= chans:
            slot, off = divmod(d * chans, share_rows)
            part = gw_all[slot, off:off + chans, :].astype(F32)
        else:
            per = chans // share_rows
            part = gw_all[d * per:(d + 1) * per].astype(F32).reshape(chans, depth)
        gw_out[pl.ds(d, chans, stride=chans), :] = part

    def finish(p):
        wait_send(bt_all, bt_s, bt_r, me, p)
        wait_send(gb_all, gb_s, gb_r, me, p)
        wait_send(gr_send, gr_s, gr_r, p, p)
        wait_send(gw_send, gw_s, gw_r, p, p)
        wait_send(gw_all, ga_s, ga_r, me, p)
    each_peer(finish)


def body(n, left, right, grad, weight, bias):
    seqs = left.shape[0]
    rows, residues, depth = grad.shape
    width = weight.shape[0]
    chans = left.shape[1] // rows
    inner = chans * seqs
    vmem = pl.BlockSpec(memory_space=pltpu.VMEM)
    sem = pltpu.SemaphoreType.DMA((n,))
    blocks = max(residues // 128, 1)
    acc_shape = (inner, rows * depth) if blocks > 1 else (8, 128)
    pair, gl, gr, gw, gb = pl.pallas_call(
        functools.partial(kernel, n),
        out_shape=(
            jax.ShapeDtypeStruct((rows, residues, depth), BF16),
            jax.ShapeDtypeStruct((seqs, rows * chans), F32),
            jax.ShapeDtypeStruct((seqs, rows * chans), F32),
            jax.ShapeDtypeStruct((width, depth), F32),
            jax.ShapeDtypeStruct((1, depth), F32),
        ),
        in_specs=[vmem] * 5,
        out_specs=[vmem] * 5,
        scratch_shapes=[
            pltpu.VMEM((width, depth), F32),
            pltpu.VMEM((chans, chans * depth), BF16),
            pltpu.VMEM((inner, rows * depth), BF16),
            pltpu.VMEM((rows * seqs, chans * depth), BF16),
            pltpu.VMEM(acc_shape, F32),
            pltpu.VMEM((n, rows, inner), BF16),
            pltpu.VMEM((n, 8, depth), F32),
            pltpu.VMEM((n, rows, inner), BF16),
            pltpu.VMEM((n, rows, inner), BF16),
            pltpu.VMEM((n, width // n, depth), BF16),
            pltpu.VMEM((n, width // n, depth), BF16),
            pltpu.VMEM((n, width // n, depth), BF16),
        ] + [sem] * 10,
        compiler_params=pltpu.CompilerParams(
            collective_id=0, has_side_effects=True, vmem_limit_bytes=56 * 1024 * 1024),
    )(left, right, grad, weight, bias.reshape(1, depth))
    return pair, gl, gr, gw, gb.reshape(depth)


def solution(mesh):
    in_specs = (P("groups", "row"), P("groups", "row"), P(("groups", "row"), None, None), P(), P())
    out_specs = (
        P(("groups", "row"), None, None),
        P("groups", "row"),
        P("groups", "row"),
        P("groups", None),
        P("groups"),
    )
    return jax.shard_map(
        functools.partial(body, mesh.shape["row"]),
        mesh=mesh, in_specs=in_specs, out_specs=out_specs, check_vma=False)
```

time: 194 us -> 41 us (0.21); the launches traced: 191 us -> 40.5 us
  waiting for transfers between devices: 92.3 us -> 0 us
  blocking collectives: 53 us -> 0 us
  Pallas kernels: 0 us -> 34.8 us
  between operations: 14.2 us -> 0.65 us
  local copies, waits for them, and re-layouts: 17.7 us -> 5.04 us
  matrix products: 9.89 us -> 0 us
  other arithmetic: 3.94 us -> 0 us
    reduce_scatter x1 -> x0, waiting for transfers between devices: 55.4 us -> none  [body(): lax.psum_scatter(partial_rows, 'row', scatter_dimension=1, tiled=True)]
    psum x1 -> x0, waiting for transfers between devices: 36.9 us -> none  [body(): weight_total, bias_total = lax.psum((grad_weight_acc, bias_local), 'row')]
    pallas_call x0 -> x1, Pallas kernels: none -> 34.8 us  [body(): pl.pallas_call(functools.partial(kernel, n), out_shape=(jax.ShapeDtypeStr...]
    psum x1 -> x0, blocking collectives: 29.1 us -> none  [body(): weight_total, bias_total = lax.psum((grad_weight_acc, bias_local), 'row')]
    all_gather x1 -> x0, blocking collectives: 23.9 us -> none  [body(): right_collected = lax.all_gather(right_alignment, 'row', axis=1, tiled=True)]
    dot_general x6 -> x0, matrix products: 9.89 us -> none  [the longest x1 3.07 us: column_step(): jnp.dot(outer, weight, preferred_element_type=jnp.float32) + bias_f]
    reshape x7 -> x0, local copies, waits for them, and re-layouts: 7.02 us -> none  [the longest x1 3.36 us: body(): grad_right_acc.reshape(sequence_count, grand_count * channel_total)]
    mul x4 -> x0, other arithmetic: 3.79 us -> none  [the longest x1 1.87 us: body(): weight_total * inv_total]
  transfers between devices with their start and end apart: 2 -> 0, of which waited for: 2 -> 0; matrix products, arithmetic and copies ran while one was open for 12% -> 0% of each run, Pallas kernels for 0% -> 0%
where the time goes in v1:
time: 41 us; the launch traced here: 40.5 us
  Pallas kernels  34.8 us (85%)
  local copies, waits for them, and re-layouts  5.04 us (12%)
  between operations  0.65 us (2%)
    pallas_call x1, Pallas kernels, body(): pl.pallas_call(functools.partial(kernel, n), out_shape=(jax.ShapeDtypeStr...  34.8 us
    unnamed x11, local copies, waits for them, and re-layouts  5.04 us

profile of v1, /device:TPU:1, one launch (start us, length us, event | category | flops | bytes accessed | tf_op | source)
XLA Modules:
  0.0 40.5 jit_solution(1723187585327273313)
XLA Ops:
  0.6 34.8 %shard_map.92 = (bf16[8,128,128]{2,1,0:T(8,128)(2,1)}, f32[32,256]{1,0:T(8,128)}, f32[32,256]{1,0:T(8,128)}, f32[1024,128]{1,0:T(8,128)}, f32[1,128]{1,0:T(1,128)}) custom-call(bf16[32,256]{1,0:T(8,128)(2,1)} %left.1, bf16[32,256]{1,0:T(8,128)(2,1)} %right.1, bf16[8,128,128]{2,1,0:T(8,128)(2,1)} %grad.1, bf16[1024,128]{1,0:T(8,128)(2,1)} %weight.1, ...), custom_call_target="tpu_custom_call" | custom-call | tf_op jit(solution)/shard_map/pallas_call | solution.py:234
  35.4 0.0 copy-start
  35.5 1.7 %copy.15 = bf16[8,128,128]{2,1,0:T(8,128)(2,1)} copy(bf16[8,128,128]{2,1,0:T(8,128)(2,1)} %get-tuple-element.20) | data formatting | bytes 524288
  37.2 0.0 copy-start.1
  37.2 1.4 %copy.16 = f32[32,256]{1,0:T(8,128)} copy(f32[32,256]{1,0:T(8,128)} %get-tuple-element.21) | data formatting | bytes 65536
  38.6 0.0 copy-done.1
  38.6 0.6 %copy.17 = f32[32,256]{1,0:T(8,128)} copy(f32[32,256]{1,0:T(8,128)S(1)} %copy-done.1) | data formatting | bytes 65536
  39.2 0.0 copy-done
  39.2 0.0 copy-start.2
  39.2 0.8 %copy.18 = f32[1024,128]{1,0:T(8,128)} copy(f32[1024,128]{1,0:T(8,128)S(1)} %copy-done) | data formatting | bytes 1048576
  40.0 0.0 copy-done.2
  40.0 0.5 %copy.19 = f32[128]{0:T(128)} copy(f32[128]{0:T(128)S(1)} %bitcast.3) | data formatting | bytes 1024
Async XLA Ops:
  35.4 3.7 %copy-start = (f32[1024,128]{1,0:T(8,128)S(1)}, f32[1024,128]{1,0:T(8,128)}, u32[]{:S(2)}) copy-start(f32[1024,128]{1,0:T(8,128)} %get-tuple-element.23) | copy-start | bytes 1572868
  37.2 1.4 %copy-start.1 = (f32[32,256]{1,0:T(8,128)S(1)}, f32[32,256]{1,0:T(8,128)}, u32[]{:S(2)}) copy-start(f32[32,256]{1,0:T(8,128)} %get-tuple-element.22) | copy-start | bytes 98308
  39.2 0.8 %copy-start.2 = (f32[1,128]{1,0:T(1,128)S(1)}, f32[1,128]{1,0:T(1,128)}, u32[]{:S(2)}) copy-start(f32[1,128]{1,0:T(1,128)} %get-tuple-element.14) | copy-start | bytes 1540

commit v2 on v1

v2 whole, which is shorter than its diff:
```python
import functools

import jax
import jax.numpy as jnp
from jax import lax
from jax.experimental import pallas as pl
from jax.experimental.pallas import tpu as pltpu
from jax.sharding import PartitionSpec as P

F32, BF16 = jnp.float32, jnp.bfloat16
NN = (((1,), (0,)), ((), ()))
NT = (((1,), (1,)), ((), ()))
TN = (((0,), (0,)), ((), ()))


def dot(x, y, dims=NN):
    return lax.dot_general(x, y, dims, preferred_element_type=F32)


def kernel(
    n, left, right, grad, weight, bias,
    pair_out, gl_out, gr_out, gw_out, gb_out,
    weight_f, weight_r, t_mat, u_mat, u_acc,
    bt_all, gb_own, gb_sib, gb_all, gr_part, gr_sib, gr_send, gr_recv,
    gw_part, gw_sib, gw_send, gw_recv, gw_all,
    bt_s, bt_r, bt_f, gb_s, gb_r, gr_s, gr_r, gw_s, gw_r, ga_s, ga_r, ga_f, sib_s, sib_r,
):
    seqs = left.shape[0]
    rows, residues, depth = grad.shape
    chans = left.shape[1] // rows
    inner = chans * seqs
    span = min(128, residues)
    blocks = residues // span
    chips = n // 2
    me = lax.axis_index("row")
    chip, core = me // 2, lax.rem(me, 2)
    other = 1 - core
    sibling = chip * 2 + other

    def each_chip(action):
        def step(k, carry):
            action(lax.rem(chip + k, chips))
            return carry
        lax.fori_loop(1, chips, step, 0)

    def each_block(action):
        if blocks == 1:
            action(0)
        else:
            def step(k, carry):
                action(pl.multiple_of(k * span, span))
                return carry
            lax.fori_loop(0, blocks, step, 0)

    def copy(src, dst, sent, received, device):
        return pltpu.make_async_remote_copy(
            src_ref=src, dst_ref=dst, send_sem=sent, recv_sem=received,
            device_id={"row": device}, device_id_type=pl.DeviceIdType.MESH)

    def share(src, dst, sent, received, p):
        return copy(src.at[p], dst.at[chip], sent.at[p], received.at[chip], p * 2 + core)

    def share_in(src, dst, sent, received, p):
        return copy(src.at[p], dst.at[p], sent.at[p], received.at[p], p * 2 + core)

    def spread_to(buf, sent, received, p):
        mine = buf.at[core, chip]
        return copy(mine, mine, sent.at[p], received.at[core, chip], p * 2 + core)

    def spread_in(buf, sent, received, p):
        slot = buf.at[core, p]
        return copy(slot, slot, sent.at[p], received.at[core, p], p * 2 + core)

    def forward(buf, sent, received, p):
        slot = buf.at[core, p]
        return copy(slot, slot, sent.at[p], received.at[core, p], sibling)

    def forward_in(buf, sent, received, p):
        slot = buf.at[other, p]
        return copy(slot, slot, sent.at[p], received.at[other, p], sibling)

    def gather_start(buf, sent, received, forwarded):
        each_chip(lambda p: spread_to(buf, sent, received, p).start())
        forward(buf, forwarded, received, chip).start()

    def gather_end(buf, sent, received, forwarded):
        def arrive(p):
            spread_in(buf, sent, received, p).wait_recv()
            forward(buf, forwarded, received, p).start()
        each_chip(arrive)
        forward_in(buf, forwarded, received, chip).wait_recv()
        each_chip(lambda p: forward_in(buf, forwarded, received, p).wait_recv())

    def gather_sent(buf, sent, received, forwarded):
        each_chip(lambda p: spread_to(buf, sent, received, p).wait_send())
        each_chip(lambda p: forward(buf, forwarded, received, p).wait_send())
        forward(buf, forwarded, received, chip).wait_send()

    barrier = pltpu.get_barrier_semaphore()

    def greet(device):
        pl.semaphore_signal(
            barrier, inc=1, device_id={"row": device}, device_id_type=pl.DeviceIdType.MESH)
    each_chip(lambda p: greet(p * 2 + core))
    greet(sibling)

    lane_s = lax.broadcasted_iota(jnp.int32, (seqs, inner), 1) % seqs
    pick = (lane_s == lax.broadcasted_iota(jnp.int32, (seqs, inner), 0)).astype(BF16)
    lane_d = lax.broadcasted_iota(jnp.int32, (rows * chans, inner), 1) // seqs
    row_d = lax.broadcasted_iota(jnp.int32, (rows * chans, inner), 0) % chans
    own = lane_d == row_d
    spread = jnp.where(own, dot(right[...], pick, TN), 0.0)
    bt_all[core, chip] = jnp.sum(spread.reshape(rows, chans, inner), axis=1).astype(BF16)

    pl.semaphore_wait(barrier, chips)
    gather_start(bt_all, bt_s, bt_r, bt_f)

    gb = jnp.zeros((8, depth), F32)
    for i in range(rows):
        gb = gb + jnp.sum(grad[i].astype(F32).reshape(residues // 8, 8, depth), axis=0)
    gb_own[...] = gb
    gb_copy = copy(gb_own, gb_sib, sib_s.at[0], sib_r.at[0], sibling)
    gb_copy.start()

    a = jnp.concatenate([left[:, i * chans:(i + 1) * chans] for i in range(rows)], axis=0)
    weight_f[...] = weight[...].astype(F32)
    for d in range(chans):
        weight_r[:, d * depth:(d + 1) * depth] = weight_f[
            pl.ds(d, chans, stride=chans), :].astype(BF16)

    for d in range(chans):
        t = dot(a, weight_r[:, d * depth:(d + 1) * depth]).astype(BF16)
        for i in range(rows):
            t_mat[d * seqs:(d + 1) * seqs, i * depth:(i + 1) * depth] = (
                t[i * seqs:(i + 1) * seqs])

    def grad_of(start):
        return jnp.concatenate(
            [grad[i, pl.ds(start, span), :] for i in range(rows)], axis=1)

    scale = 1.0 / seqs
    pairs = span // (2 * rows)

    def right_share(start):
        part = dot(grad_of(start), t_mat[...], NT) * scale
        for k in range(pairs):
            for c in range(2):
                first = (2 * k + c) * rows
                gr_part[c, start // (2 * rows) + k] = part[first:first + rows]
    each_block(right_share)
    gr_copy = copy(gr_part.at[other], gr_sib, sib_s.at[1], sib_r.at[1], sibling)
    gr_copy.start()

    gather_end(bt_all, bt_s, bt_r, bt_f)

    def right_of(start):
        first = start // (2 * rows)
        halves = [bt_all[c, pl.ds(first, pairs)].astype(F32) for c in range(2)]
        return jnp.stack(halves, axis=1).reshape(span, inner)

    def put_u(u):
        for d in range(chans):
            for i in range(rows):
                u_mat[i * seqs:(i + 1) * seqs, d * depth:(d + 1) * depth] = u[
                    d * seqs:(d + 1) * seqs, i * depth:(i + 1) * depth].astype(BF16)

    def u_of(start):
        return dot(right_of(start).T.astype(BF16), grad_of(start))

    if blocks == 1:
        put_u(u_of(0))
    else:
        u_acc[...] = jnp.zeros_like(u_acc)

        def add_u(start):
            u_acc[...] += u_of(start)
        each_block(add_u)
        put_u(u_acc)

    share_rows = gw_send.shape[1]
    a_t = a.astype(F32).T.astype(BF16)
    gw_scale = 1.0 / (seqs * residues)
    for d in range(chans):
        part = (dot(a_t, u_mat[:, d * depth:(d + 1) * depth]) * gw_scale)
        half, local = divmod(d, chans // 2)
        if share_rows >= chans:
            slot, off = divmod(local * chans, share_rows)
            gw_part[half, slot, off:off + chans, :] = part
        else:
            per = chans // share_rows
            gw_part[half, local * per:(local + 1) * per] = part.reshape(per, share_rows, depth)
    gw_copy = copy(gw_part.at[other], gw_sib, sib_s.at[2], sib_r.at[2], sibling)
    gw_copy.start()

    gr_copy.wait_recv()

    def chip_gr(p):
        gr_send[p] = (gr_part[core, p] + gr_sib[p]).astype(BF16)
        share(gr_send, gr_recv, gr_s, gr_r, p).start()

    gw_copy.wait_recv()

    def chip_gw(p):
        gw_send[p] = (gw_part[core, p] + gw_sib[p]).astype(BF16)
        share(gw_send, gw_recv, gw_s, gw_r, p).start()
    each_chip(chip_gw)
    each_chip(chip_gr)

    gb_copy.wait_recv()
    gb_all[chip] = gb_own[...] + gb_sib[...]
    each_chip(lambda p: copy(
        gb_all.at[chip], gb_all.at[chip], gb_s.at[p], gb_r.at[chip], p * 2 + core).start())

    bias_f = jnp.broadcast_to(bias[...].astype(F32), (span, depth))

    def pair_of(start):
        pair = dot(right_of(start).astype(BF16), t_mat[...])
        for i in range(rows):
            pair_out[i, pl.ds(start, span), :] = (
                pair[:, i * depth:(i + 1) * depth] * scale + bias_f).astype(BF16)
    each_block(pair_of)

    def add_in(recv, sent, received, send_buf):
        def step(k, acc):
            p = lax.rem(chip + k, chips)
            share_in(send_buf, recv, sent, received, p).wait_recv()
            return acc + recv[p].astype(F32)
        return step

    total = lax.fori_loop(
        1, chips, add_in(gw_recv, gw_s, gw_r, gw_send), gw_part[core, chip] + gw_sib[chip])
    gw_all[core, chip] = total.astype(BF16)
    gather_start(gw_all, ga_s, ga_r, ga_f)

    gl = dot(u_mat[...], weight_r[...], NT) * scale
    for i in range(rows):
        gl_out[:, i * chans:(i + 1) * chans] = gl[i * seqs:(i + 1) * seqs]

    gr = lax.fori_loop(
        1, chips, add_in(gr_recv, gr_s, gr_r, gr_send), gr_part[core, chip] + gr_sib[chip])
    wide = jnp.broadcast_to(gr[:, None, :], (rows, chans, inner)).reshape(rows * chans, inner)
    wide = jnp.where(own, wide, 0.0)
    high = wide.astype(BF16)
    low = (wide - high.astype(F32)).astype(BF16)
    gr_out[...] = dot(pick, high, NT) + dot(pick, low, NT)

    each_chip(lambda p: share_in(gb_all, gb_all, gb_s, gb_r, p).wait_recv())
    gb_total = lax.fori_loop(
        0, chips, lambda k, acc: acc + gb_all[k], jnp.zeros((8, depth), F32))
    gb_out[...] = jnp.sum(gb_total, axis=0, keepdims=True) * (1.0 / residues)

    gather_end(gw_all, ga_s, ga_r, ga_f)
    for d in range(chans):
        half, local = divmod(d, chans // 2)
        if share_rows >= chans:
            slot, off = divmod(local * chans, share_rows)
            part = gw_all[half, slot, off:off + chans, :].astype(F32)
        else:
            per = chans // share_rows
            part = gw_all[half, local * per:(local + 1) * per].astype(F32).reshape(chans, depth)
        gw_out[pl.ds(d, chans, stride=chans), :] = part

    gather_sent(bt_all, bt_s, bt_r, bt_f)
    gather_sent(gw_all, ga_s, ga_r, ga_f)
    gb_copy.wait_send()
    gr_copy.wait_send()
    gw_copy.wait_send()

    def finish(p):
        share(gr_send, gr_recv, gr_s, gr_r, p).wait_send()
        share(gw_send, gw_recv, gw_s, gw_r, p).wait_send()
        copy(gb_all.at[chip], gb_all.at[chip], gb_s.at[p], gb_r.at[chip], p * 2 + core).wait_send()
    each_chip(finish)


def body(n, left, right, grad, weight, bias):
    seqs = left.shape[0]
    rows, residues, depth = grad.shape
    width = weight.shape[0]
    chans = left.shape[1] // rows
    inner = chans * seqs
    chips = n // 2
    vmem = pl.BlockSpec(memory_space=pltpu.VMEM)
    sem = pltpu.SemaphoreType.DMA((chips,))
    sem2 = pltpu.SemaphoreType.DMA((2, chips))
    blocks = max(residues // 128, 1)
    acc_shape = (inner, rows * depth) if blocks > 1 else (8, 128)
    pair, gl, gr, gw, gb = pl.pallas_call(
        functools.partial(kernel, n),
        out_shape=(
            jax.ShapeDtypeStruct((rows, residues, depth), BF16),
            jax.ShapeDtypeStruct((seqs, rows * chans), F32),
            jax.ShapeDtypeStruct((seqs, rows * chans), F32),
            jax.ShapeDtypeStruct((width, depth), F32),
            jax.ShapeDtypeStruct((1, depth), F32),
        ),
        in_specs=[vmem] * 5,
        out_specs=[vmem] * 5,
        scratch_shapes=[
            pltpu.VMEM((width, depth), F32),
            pltpu.VMEM((chans, chans * depth), BF16),
            pltpu.VMEM((inner, rows * depth), BF16),
            pltpu.VMEM((rows * seqs, chans * depth), BF16),
            pltpu.VMEM(acc_shape, F32),
            pltpu.VMEM((2, chips, rows, inner), BF16),
            pltpu.VMEM((8, depth), F32),
            pltpu.VMEM((8, depth), F32),
            pltpu.VMEM((chips, 8, depth), F32),
            pltpu.VMEM((2, chips, rows, inner), F32),
            pltpu.VMEM((chips, rows, inner), F32),
            pltpu.VMEM((chips, rows, inner), BF16),
            pltpu.VMEM((chips, rows, inner), BF16),
            pltpu.VMEM((2, chips, width // n, depth), F32),
            pltpu.VMEM((chips, width // n, depth), F32),
            pltpu.VMEM((chips, width // n, depth), BF16),
            pltpu.VMEM((chips, width // n, depth), BF16),
            pltpu.VMEM((2, chips, width // n, depth), BF16),
            sem, sem2, sem, sem, sem, sem, sem, sem, sem, sem, sem2, sem,
            pltpu.SemaphoreType.DMA((3,)),
            pltpu.SemaphoreType.DMA((3,)),
        ],
        compiler_params=pltpu.CompilerParams(
            collective_id=0, has_side_effects=True, vmem_limit_bytes=56 * 1024 * 1024),
    )(left, right, grad, weight, bias.reshape(1, depth))
    return pair, gl, gr, gw, gb.reshape(depth)


def solution(mesh):
    in_specs = (P("groups", "row"), P("groups", "row"), P(("groups", "row"), None, None), P(), P())
    out_specs = (
        P(("groups", "row"), None, None),
        P("groups", "row"),
        P("groups", "row"),
        P("groups", None),
        P("groups"),
    )
    return jax.shard_map(
        functools.partial(body, mesh.shape["row"]),
        mesh=mesh, in_specs=in_specs, out_specs=out_specs, check_vma=False)
```

time: 41 us -> 35.2 us (0.86)
  Pallas kernels: 34.8 us -> 29.3 us
    pallas_call x1, Pallas kernels: 34.8 us -> 29.3 us  [body(): pl.pallas_call(functools.partial(kernel, n), out_shape=(jax.ShapeDtypeStr...]
where the time goes in v2:
time: 35.2 us; the launch traced here: 35 us
  Pallas kernels  29.3 us (83%)
  local copies, waits for them, and re-layouts  5.04 us (14%)
  between operations  0.65 us (2%)
    pallas_call x1, Pallas kernels, body(): pl.pallas_call(functools.partial(kernel, n), out_shape=(jax.ShapeDtypeStr...  29.3 us
    unnamed x11, local copies, waits for them, and re-layouts  5.04 us

profile of v2, /device:TPU:1, one launch (start us, length us, event | category | flops | bytes accessed | tf_op | source)
XLA Modules:
  0.0 35.0 jit_solution(8086447923935092023)
XLA Ops:
  0.6 29.3 %shard_map.92 = (bf16[8,128,128]{2,1,0:T(8,128)(2,1)}, f32[32,256]{1,0:T(8,128)}, f32[32,256]{1,0:T(8,128)}, f32[1024,128]{1,0:T(8,128)}, f32[1,128]{1,0:T(1,128)}) custom-call(bf16[32,256]{1,0:T(8,128)(2,1)} %left.1, bf16[32,256]{1,0:T(8,128)(2,1)} %right.1, bf16[8,128,128]{2,1,0:T(8,128)(2,1)} %grad.1, bf16[1024,128]{1,0:T(8,128)(2,1)} %weight.1, ...), custom_call_target="tpu_custom_call" | custom-call | tf_op jit(solution)/shard_map/pallas_call | solution.py:288
  30.0 0.0 copy-start
  30.0 1.7 %copy.15 = bf16[8,128,128]{2,1,0:T(8,128)(2,1)} copy(bf16[8,128,128]{2,1,0:T(8,128)(2,1)} %get-tuple-element.20) | data formatting | bytes 524288
  31.7 0.0 copy-start.1
  31.7 1.4 %copy.16 = f32[32,256]{1,0:T(8,128)} copy(f32[32,256]{1,0:T(8,128)} %get-tuple-element.21) | data formatting | bytes 65536
  33.1 0.0 copy-done.1
  33.1 0.6 %copy.17 = f32[32,256]{1,0:T(8,128)} copy(f32[32,256]{1,0:T(8,128)S(1)} %copy-done.1) | data formatting | bytes 65536
  33.7 0.0 copy-done
  33.7 0.0 copy-start.2
  33.7 0.8 %copy.18 = f32[1024,128]{1,0:T(8,128)} copy(f32[1024,128]{1,0:T(8,128)S(1)} %copy-done) | data formatting | bytes 1048576
  34.5 0.0 copy-done.2
  34.5 0.5 %copy.19 = f32[128]{0:T(128)} copy(f32[128]{0:T(128)S(1)} %bitcast.3) | data formatting | bytes 1024
Async XLA Ops:
  30.0 3.7 %copy-start = (f32[1024,128]{1,0:T(8,128)S(1)}, f32[1024,128]{1,0:T(8,128)}, u32[]{:S(2)}) copy-start(f32[1024,128]{1,0:T(8,128)} %get-tuple-element.23) | copy-start | bytes 1572868
  31.7 1.4 %copy-start.1 = (f32[32,256]{1,0:T(8,128)S(1)}, f32[32,256]{1,0:T(8,128)}, u32[]{:S(2)}) copy-start(f32[32,256]{1,0:T(8,128)} %get-tuple-element.22) | copy-start | bytes 98308
  33.7 0.8 %copy-start.2 = (f32[1,128]{1,0:T(1,128)S(1)}, f32[1,128]{1,0:T(1,128)}, u32[]{:S(2)}) copy-start(f32[1,128]{1,0:T(1,128)} %get-tuple-element.14) | copy-start | bytes 1540

commit v3 on v2

--- a/solution.py
+++ b/solution.py
@@ -112,15 +112,11 @@
     spread = jnp.where(own, dot(right[...], pick, TN), 0.0)
     bt_all[core, chip] = jnp.sum(spread.reshape(rows, chans, inner), axis=1).astype(BF16)
 
-    pl.semaphore_wait(barrier, chips)
-    gather_start(bt_all, bt_s, bt_r, bt_f)
-
     gb = jnp.zeros((8, depth), F32)
     for i in range(rows):
         gb = gb + jnp.sum(grad[i].astype(F32).reshape(residues // 8, 8, depth), axis=0)
     gb_own[...] = gb
     gb_copy = copy(gb_own, gb_sib, sib_s.at[0], sib_r.at[0], sibling)
-    gb_copy.start()
 
     a = jnp.concatenate([left[:, i * chans:(i + 1) * chans] for i in range(rows)], axis=0)
     weight_f[...] = weight[...].astype(F32)
@@ -148,10 +144,21 @@
                 first = (2 * k + c) * rows
                 gr_part[c, start // (2 * rows) + k] = part[first:first + rows]
     each_block(right_share)
+    pl.semaphore_wait(barrier, chips)
+    gather_start(bt_all, bt_s, bt_r, bt_f)
+
+    gb_copy.start()
     gr_copy = copy(gr_part.at[other], gr_sib, sib_s.at[1], sib_r.at[1], sibling)
     gr_copy.start()
 
     gather_end(bt_all, bt_s, bt_r, bt_f)
+    gr_copy.wait_recv()
+
+    def chip_gr(p):
+        gr_send[p] = (gr_part[core, p] + gr_sib[p]).astype(BF16)
+        share(gr_send, gr_recv, gr_s, gr_r, p).start()
+
+    each_chip(chip_gr)
 
     def right_of(start):
         first = start // (2 * rows)
@@ -192,19 +199,12 @@
     gw_copy = copy(gw_part.at[other], gw_sib, sib_s.at[2], sib_r.at[2], sibling)
     gw_copy.start()
 
-    gr_copy.wait_recv()
-
-    def chip_gr(p):
-        gr_send[p] = (gr_part[core, p] + gr_sib[p]).astype(BF16)
-        share(gr_send, gr_recv, gr_s, gr_r, p).start()
-
     gw_copy.wait_recv()
 
     def chip_gw(p):
         gw_send[p] = (gw_part[core, p] + gw_sib[p]).astype(BF16)
         share(gw_send, gw_recv, gw_s, gw_r, p).start()
     each_chip(chip_gw)
-    each_chip(chip_gr)
 
     gb_copy.wait_recv()
     gb_all[chip] = gb_own[...] + gb_sib[...]
@@ -271,6 +271,17 @@
         share(gw_send, gw_recv, gw_s, gw_r, p).wait_send()
         copy(gb_all.at[chip], gb_all.at[chip], gb_s.at[p], gb_r.at[chip], p * 2 + core).wait_send()
     each_chip(finish)
+
+
+def hand_over(*refs):
+    sems = refs[-1]
+    count = (len(refs) - 1) // 2
+    copies = [
+        pltpu.make_async_copy(refs[k], refs[count + k], sems.at[k]) for k in range(count)]
+    for one in copies:
+        one.start()
+    for one in copies:
+        one.wait()
 
 
 def body(n, left, right, grad, weight, bias):
@@ -285,7 +296,7 @@
     sem2 = pltpu.SemaphoreType.DMA((2, chips))
     blocks = max(residues // 128, 1)
     acc_shape = (inner, rows * depth) if blocks > 1 else (8, 128)
-    pair, gl, gr, gw, gb = pl.pallas_call(
+    outs = pl.pallas_call(
         functools.partial(kernel, n),
         out_shape=(
             jax.ShapeDtypeStruct((rows, residues, depth), BF16),
@@ -322,6 +333,14 @@
         compiler_params=pltpu.CompilerParams(
             collective_id=0, has_side_effects=True, vmem_limit_bytes=56 * 1024 * 1024),
     )(left, right, grad, weight, bias.reshape(1, depth))
+    hbm = pl.BlockSpec(memory_space=pltpu.VMEM)
+    pair, gl, gr, gw, gb = pl.pallas_call(
+        hand_over,
+        out_shape=tuple(jax.ShapeDtypeStruct(x.shape, x.dtype) for x in outs),
+        in_specs=[pl.BlockSpec(memory_space=pl.ANY)] * 5,
+        out_specs=[hbm] * 5,
+        scratch_shapes=[pltpu.SemaphoreType.DMA((5,))],
+    )(*outs)
     return pair, gl, gr, gw, gb.reshape(depth)
 
 

time: 35.2 us -> 31 us (0.88)
  local copies, waits for them, and re-layouts: 5.04 us -> 0 us
  Pallas kernels: 29.3 us -> 30.2 us
    unnamed x11 -> x0, local copies, waits for them, and re-layouts: 5.04 us -> none
    pallas_call x0 -> x1, Pallas kernels: none -> 2.1 us  [body(): pl.pallas_call(hand_over, out_shape=tuple((jax.ShapeDtypeStruct(x.shape,...]
    pallas_call x1, Pallas kernels: 29.3 us -> 28.1 us  [body(): pl.pallas_call(functools.partial(kernel, n), out_shape=(jax.ShapeDtypeStr...]
where the time goes in v3:
time: 31 us; the launch traced here: 30.9 us
  Pallas kernels  30.2 us (97%)
  between operations  0.64 us (2%)
    pallas_call x1, Pallas kernels, body(): pl.pallas_call(functools.partial(kernel, n), out_shape=(jax.ShapeDtypeStr...  28.1 us
    pallas_call x1, Pallas kernels, body(): pl.pallas_call(hand_over, out_shape=tuple((jax.ShapeDtypeStruct(x.shape,...  2.1 us

profile of v3, /device:TPU:1, one launch (start us, length us, event | category | flops | bytes accessed | tf_op | source)
XLA Modules:
  0.0 30.9 jit_solution(15458816679508597021)
XLA Ops:
  0.6 28.1 %shard_map.92 = (bf16[8,128,128]{2,1,0:T(8,128)(2,1)}, f32[32,256]{1,0:T(8,128)}, f32[32,256]{1,0:T(8,128)}, f32[1024,128]{1,0:T(8,128)}, f32[1,128]{1,0:T(1,128)}) custom-call(bf16[32,256]{1,0:T(8,128)(2,1)} %left.1, bf16[32,256]{1,0:T(8,128)(2,1)} %right.1, bf16[8,128,128]{2,1,0:T(8,128)(2,1)} %grad.1, bf16[1024,128]{1,0:T(8,128)(2,1)} %weight.1, ...), custom_call_target="tpu_custom_call" | custom-call | tf_op jit(solution)/shard_map/pallas_call | solution.py:299
  28.8 2.1 %shard_map.93 = (bf16[8,128,128]{2,1,0:T(8,128)(2,1)}, f32[32,256]{1,0:T(8,128)}, f32[32,256]{1,0:T(8,128)}, f32[1024,128]{1,0:T(8,128)}, f32[1,128]{1,0:T(1,128)}) custom-call(bf16[8,128,128]{2,1,0:T(8,128)(2,1)} %get-tuple-element.15.refs_0_, f32[32,256]{1,0:T(8,128)} %get-tuple-element.16.refs_1_, f32[32,256]{1,0:T(8,128)} %get-tuple-element.17.refs_2_, ...), custom_call_target="tpu_custom_call" | custom-call | tf_op jit(solution)/shard_map/pallas_call | solution.py:337

commit v4 on v3

--- a/solution.py
+++ b/solution.py
@@ -18,12 +18,13 @@
 
 
 def kernel(
-    n, left, right, grad, weight, bias,
+    n, left_in, right_in, grad_in, weight_in, bias_in,
     pair_out, gl_out, gr_out, gw_out, gb_out,
     weight_f, weight_r, t_mat, u_mat, u_acc,
     bt_all, gb_own, gb_sib, gb_all, gr_part, gr_sib, gr_send, gr_recv,
     gw_part, gw_sib, gw_send, gw_recv, gw_all,
     bt_s, bt_r, bt_f, gb_s, gb_r, gr_s, gr_r, gw_s, gw_r, ga_s, ga_r, ga_f, sib_s, sib_r,
+    left, right, grad, weight, bias, load_s,
 ):
     seqs = left.shape[0]
     rows, residues, depth = grad.shape
@@ -104,6 +105,16 @@
     each_chip(lambda p: greet(p * 2 + core))
     greet(sibling)
 
+    loads = [
+        pltpu.make_async_copy(source, target, load_s.at[k])
+        for k, (source, target) in enumerate((
+            (right_in, right), (weight_in, weight), (left_in, left), (grad_in, grad),
+            (bias_in, bias)))]
+    for load in loads:
+        load.start()
+
+    loads[0].wait()
+
     lane_s = lax.broadcasted_iota(jnp.int32, (seqs, inner), 1) % seqs
     pick = (lane_s == lax.broadcasted_iota(jnp.int32, (seqs, inner), 0)).astype(BF16)
     lane_d = lax.broadcasted_iota(jnp.int32, (rows * chans, inner), 1) // seqs
@@ -112,23 +123,30 @@
     spread = jnp.where(own, dot(right[...], pick, TN), 0.0)
     bt_all[core, chip] = jnp.sum(spread.reshape(rows, chans, inner), axis=1).astype(BF16)
 
+    pl.semaphore_wait(barrier, chips)
+    gather_start(bt_all, bt_s, bt_r, bt_f)
+
+    loads[1].wait()
+    loads[2].wait()
+    a = jnp.concatenate([left[:, i * chans:(i + 1) * chans] for i in range(rows)], axis=0)
+    weight_f[...] = weight[...].astype(F32)
+    for d in range(chans):
+        weight_r[:, d * depth:(d + 1) * depth] = weight_f[
+            pl.ds(d, chans, stride=chans), :].astype(BF16)
+
+    for d in range(chans):
+        t = dot(a, weight_r[:, d * depth:(d + 1) * depth]).astype(BF16)
+        for i in range(rows):
+            t_mat[d * seqs:(d + 1) * seqs, i * depth:(i + 1) * depth] = (
+                t[i * seqs:(i + 1) * seqs])
+
+    loads[3].wait()
+    loads[4].wait()
     gb = jnp.zeros((8, depth), F32)
     for i in range(rows):
         gb = gb + jnp.sum(grad[i].astype(F32).reshape(residues // 8, 8, depth), axis=0)
     gb_own[...] = gb
     gb_copy = copy(gb_own, gb_sib, sib_s.at[0], sib_r.at[0], sibling)
-
-    a = jnp.concatenate([left[:, i * chans:(i + 1) * chans] for i in range(rows)], axis=0)
-    weight_f[...] = weight[...].astype(F32)
-    for d in range(chans):
-        weight_r[:, d * depth:(d + 1) * depth] = weight_f[
-            pl.ds(d, chans, stride=chans), :].astype(BF16)
-
-    for d in range(chans):
-        t = dot(a, weight_r[:, d * depth:(d + 1) * depth]).astype(BF16)
-        for i in range(rows):
-            t_mat[d * seqs:(d + 1) * seqs, i * depth:(i + 1) * depth] = (
-                t[i * seqs:(i + 1) * seqs])
 
     def grad_of(start):
         return jnp.concatenate(
@@ -144,9 +162,6 @@
                 first = (2 * k + c) * rows
                 gr_part[c, start // (2 * rows) + k] = part[first:first + rows]
     each_block(right_share)
-    pl.semaphore_wait(barrier, chips)
-    gather_start(bt_all, bt_s, bt_r, bt_f)
-
     gb_copy.start()
     gr_copy = copy(gr_part.at[other], gr_sib, sib_s.at[1], sib_r.at[1], sibling)
     gr_copy.start()
@@ -305,7 +320,7 @@
             jax.ShapeDtypeStruct((width, depth), F32),
             jax.ShapeDtypeStruct((1, depth), F32),
         ),
-        in_specs=[vmem] * 5,
+        in_specs=[pl.BlockSpec(memory_space=pl.ANY)] * 5,
         out_specs=[vmem] * 5,
         scratch_shapes=[
             pltpu.VMEM((width, depth), F32),
@@ -329,6 +344,12 @@
             sem, sem2, sem, sem, sem, sem, sem, sem, sem, sem, sem2, sem,
             pltpu.SemaphoreType.DMA((3,)),
             pltpu.SemaphoreType.DMA((3,)),
+            pltpu.VMEM(left.shape, BF16),
+            pltpu.VMEM(right.shape, BF16),
+            pltpu.VMEM(grad.shape, BF16),
+            pltpu.VMEM(weight.shape, BF16),
+            pltpu.VMEM((1, depth), BF16),
+            pltpu.SemaphoreType.DMA((5,)),
         ],
         compiler_params=pltpu.CompilerParams(
             collective_id=0, has_side_effects=True, vmem_limit_bytes=56 * 1024 * 1024),

time: 31 us -> 30.2 us (0.974)
  Pallas kernels: 30.2 us -> 29.3 us
    pallas_call x1, Pallas kernels: 28.1 us -> 27.2 us  [body(): pl.pallas_call(functools.partial(kernel, n), out_shape=(jax.ShapeDtypeStr...]
where the time goes in v4:
time: 30.2 us; the launch traced here: 29.9 us
  Pallas kernels  29.3 us (97%)
  between operations  0.64 us (2%)
    pallas_call x1, Pallas kernels, body(): pl.pallas_call(functools.partial(kernel, n), out_shape=(jax.ShapeDtypeStr...  27.2 us
    pallas_call x1, Pallas kernels, body(): pl.pallas_call(hand_over, out_shape=tuple((jax.ShapeDtypeStruct(x.shape,...  2.1 us

profile of v4, /device:TPU:1, one launch (start us, length us, event | category | flops | bytes accessed | tf_op | source)
XLA Modules:
  0.0 29.9 jit_solution(3442690744796417259)
XLA Ops:
  0.6 27.2 %shard_map.92 = (bf16[8,128,128]{2,1,0:T(8,128)(2,1)}, f32[32,256]{1,0:T(8,128)}, f32[32,256]{1,0:T(8,128)}, f32[1024,128]{1,0:T(8,128)}, f32[1,128]{1,0:T(1,128)}) custom-call(bf16[32,256]{1,0:T(8,128)(2,1)} %left_in.1, bf16[32,256]{1,0:T(8,128)(2,1)} %right_in.1, bf16[8,128,128]{2,1,0:T(8,128)(2,1)} %grad_in.1, bf16[1024,128]{1,0:T(8,128)(2,1)} %weight_in.1, ...), custom_call_target="tpu_custom_call" | custom-call | tf_op jit(solution)/shard_map/pallas_call | solution.py:314
  27.8 2.1 %shard_map.93 = (bf16[8,128,128]{2,1,0:T(8,128)(2,1)}, f32[32,256]{1,0:T(8,128)}, f32[32,256]{1,0:T(8,128)}, f32[1024,128]{1,0:T(8,128)}, f32[1,128]{1,0:T(1,128)}) custom-call(bf16[8,128,128]{2,1,0:T(8,128)(2,1)} %get-tuple-element.15.refs_0_, f32[32,256]{1,0:T(8,128)} %get-tuple-element.16.refs_1_, f32[32,256]{1,0:T(8,128)} %get-tuple-element.17.refs_2_, ...), custom_call_target="tpu_custom_call" | custom-call | tf_op jit(solution)/shard_map/pallas_call | solution.py:358
